TPU v7x, 32 devices: a whole 2x2x4 slice. The times are simulated.
32 devices in a mesh: dp: 8 (over z, x), mp: 4 (over y, core).
Axes of the slice: x: 2, y: 2, z: 4, core: 2. Of those that a mesh axis runs over, the one named last changes fastest.
Arguments:
- tokens: bfloat16 [8, 2048, 1024], P('dp', 'mp'), may hold values from -6 to 6
- cotangent: bfloat16 [8, 2048, 1024], P('dp', 'mp'), may hold values from -6 to 6
- w_qkv: float32 [3, 1024, 1024], P(None, 'dp', 'mp'), may hold values from -0.1875 to 0.1875
- w_out: float32 [1024, 1024], P('mp', 'dp'), may hold values from -3 to 3
- w_up: float32 [1024, 4096], P('dp', 'mp'), may hold values from -0.1875 to 0.1875
- w_down: float32 [4096, 1024], P('mp', 'dp'), may hold values from -0.09375 to 0.09375
- gain_attn: float32 [1024], replicated, may hold values from 0.5 to 1.5
- shift_attn: float32 [1024], replicated, may hold values from -1.5 to 1.5
- gain_ffn: float32 [1024], replicated, may hold values from 0.5 to 1.5
- shift_ffn: float32 [1024], replicated, may hold values from -1.5 to 1.5
- bias_up: float32 [4096], P('mp'), may hold values from -1.5 to 1.5
- bias_down: float32 [1024], replicated, may hold values from -1.5 to 1.5
- random_blocks: int32 [8, 16, 30, 3], P('dp', 'mp'), may hold values from 1 to 30
Outputs:
- out_tokens: bfloat16 [8, 2048, 1024], P('dp', 'mp')
- grad_tokens: float32 [8, 2048, 1024], P('dp', 'mp')
- new_qkv: float32 [3, 1024, 1024], P(None, 'dp', 'mp')
- qkv_rows: float32 [3, 1024], P(None, 'dp')
- qkv_cols: float32 [3, 1024], P(None, 'mp')
- new_out: float32 [1024, 1024], P('mp', 'dp')
- out_rows: float32 [1024], P('mp')
- out_cols: float32 [1024], P('dp')
- new_up: float32 [1024, 4096], P('dp', 'mp')
- up_rows: float32 [1024], P('dp')
- up_cols: float32 [4096], P('mp')
- new_down: float32 [4096, 1024], P('mp', 'dp')
- down_rows: float32 [4096], P('mp')
- down_cols: float32 [1024], P('dp')
- grad_gain_attn: float32 [1024], replicated
- grad_shift_attn: float32 [1024], replicated
- grad_gain_ffn: float32 [1024], replicated
- grad_shift_ffn: float32 [1024], replicated
- grad_bias_up: float32 [4096], P('mp')
- grad_bias_down: float32 [1024], replicated
Inputs may be any that keep to these rules, and one draw needn't show every extreme that they name: `random_blocks`: every entry names a block of the same document other than its first and last; entries may repeat and may equal window blocks.
All inputs are finite; a program needn't handle non-finite values.
Results may differ from a plain program's by a relative error of at most 0.04.
Values may be sent and summed in bfloat16 or wider, within the bound.
No kernel may reach another device: no remote copies, remote signals or barrier semaphores. Data moves between devices by JAX's collectives and lax.ppermute only.
A program may use at most 192 MiB of HBM per device.

v0:
```python
import jax
import jax.numpy as jnp
from jax import lax
from jax.sharding import PartitionSpec as P

D = 1024
FF = 4096
BLOCK = 64
EPS_NORM = 1e-05
EPS_FACTOR = 1e-30
LEARN_RATE = 0.1
GELU_SCALE = 0.7978845608028654


def gelu_tanh(values):
    return (
        0.5 * values * (1.0 + jnp.tanh(GELU_SCALE * (values + 0.044715 * values * values * values)))
    )


def block_table(random_rows, blocks_all):
    middle = jnp.arange(1, blocks_all - 1, dtype=jnp.int32)[:, None]
    fixed = jnp.concatenate(
        [
            jnp.zeros_like(middle),
            middle - 1,
            middle,
            middle + 1,
            jnp.zeros_like(middle) + (blocks_all - 1),
        ],
        axis=1,
    )
    return jnp.concatenate([fixed, random_rows], axis=1)


def spread_rows(local_part):
    return lax.all_gather(local_part, "mp", axis=0, tiled=True)


def spread_grads(local_part):
    return lax.all_gather(local_part, "mp", axis=0, tiled=True)


def combine_heads(partial_value):
    return lax.psum_scatter(
        partial_value.astype(jnp.bfloat16), "mp", scatter_dimension=0, tiled=True
    ).astype(jnp.float32)


def combine_grads(partial_value):
    return lax.psum_scatter(
        partial_value.astype(jnp.bfloat16), "mp", scatter_dimension=0, tiled=True
    ).astype(jnp.float32)


def norm_forward(values, norm_gain, norm_shift):
    center = jnp.mean(values, axis=1, keepdims=True)
    spread = values - center
    variance = jnp.mean(spread * spread, axis=1, keepdims=True)
    inverse = lax.rsqrt(variance + EPS_NORM)
    normal = spread * inverse
    return ((normal * norm_gain + norm_shift).astype(jnp.bfloat16), normal, inverse)


def norm_backward(grad_norm, norm_gain, normal, inverse):
    scaled = grad_norm * norm_gain
    mean_plain = jnp.mean(scaled, axis=1, keepdims=True)
    mean_normal = jnp.mean(scaled * normal, axis=1, keepdims=True)
    grad_values = inverse * (scaled - mean_plain - normal * mean_normal)
    return (grad_values, jnp.sum(grad_norm * normal, axis=0), jnp.sum(grad_norm, axis=0))


def near_blocks(block_rows, key_table):
    return jnp.take(block_rows, key_table, axis=0).reshape(
        key_table.shape[0], -1, block_rows.shape[2]
    )


def attend_group(query_group, key_group, value_group, scaling):
    scores = (
        jnp.einsum("nqe,nke->nqk", query_group, key_group, preferred_element_type=jnp.float32)
        * scaling
    )
    highest = jnp.max(scores, axis=-1, keepdims=True)
    expanded = jnp.exp(scores - highest)
    summed = jnp.sum(expanded, axis=-1, keepdims=True)
    probs = (expanded / summed).astype(jnp.bfloat16)
    result = jnp.einsum("nqk,nke->nqe", probs, value_group, preferred_element_type=jnp.float32)
    return (result, highest + jnp.log(summed))


def attend_back(query_group, key_group, value_group, grad_group, log_total, scaling):
    scores = (
        jnp.einsum("nqe,nke->nqk", query_group, key_group, preferred_element_type=jnp.float32)
        * scaling
    )
    probs = jnp.exp(scores - log_total)
    grad_probs = jnp.einsum(
        "nqe,nke->nqk", grad_group, value_group, preferred_element_type=jnp.float32
    )
    center = jnp.sum(probs * grad_probs, axis=-1, keepdims=True)
    grad_score = (probs * (grad_probs - center)).astype(jnp.bfloat16)
    grad_query = (
        jnp.einsum("nqk,nke->nqe", grad_score, key_group, preferred_element_type=jnp.float32)
        * scaling
    )
    grad_key = (
        jnp.einsum("nqk,nqe->nke", grad_score, query_group, preferred_element_type=jnp.float32)
        * scaling
    )
    grad_value = jnp.einsum(
        "nqk,nqe->nke", probs.astype(jnp.bfloat16), grad_group, preferred_element_type=jnp.float32
    )
    return (grad_query, grad_key, grad_value)


def head_forward(queries, key_rows, value_rows, key_table):
    head_dim = queries.shape[1]
    blocks_all = queries.shape[0] // BLOCK
    scaling = head_dim ** (-0.5)
    query_blocks = queries.reshape(blocks_all, BLOCK, head_dim)
    key_near = near_blocks(key_rows.reshape(blocks_all, BLOCK, head_dim), key_table)
    value_near = near_blocks(value_rows.reshape(blocks_all, BLOCK, head_dim), key_table)
    out_mid, log_mid = attend_group(query_blocks[1:-1], key_near, value_near, scaling)
    query_ends = jnp.concatenate([query_blocks[0], query_blocks[-1]], axis=0)
    out_ends, log_ends = attend_group(query_ends[None], key_rows[None], value_rows[None], scaling)
    joined = jnp.concatenate([out_ends[:, :BLOCK], out_mid, out_ends[:, BLOCK:]], axis=0)
    return (joined.reshape(-1, head_dim).astype(jnp.bfloat16), log_mid, log_ends)


def head_backward(queries, key_rows, value_rows, key_table, grad_out, log_mid, log_ends):
    head_dim = queries.shape[1]
    blocks_all = queries.shape[0] // BLOCK
    scaling = head_dim ** (-0.5)
    query_blocks = queries.reshape(blocks_all, BLOCK, head_dim)
    grad_blocks = grad_out.reshape(blocks_all, BLOCK, head_dim)
    key_near = near_blocks(key_rows.reshape(blocks_all, BLOCK, head_dim), key_table)
    value_near = near_blocks(value_rows.reshape(blocks_all, BLOCK, head_dim), key_table)
    mid_query, mid_key, mid_value = attend_back(
        query_blocks[1:-1], key_near, value_near, grad_blocks[1:-1], log_mid, scaling
    )
    segment_ids = key_table.reshape(-1)
    key_sum = jax.ops.segment_sum(
        mid_key.reshape(-1, BLOCK, head_dim), segment_ids, num_segments=blocks_all
    ).reshape(-1, head_dim)
    value_sum = jax.ops.segment_sum(
        mid_value.reshape(-1, BLOCK, head_dim), segment_ids, num_segments=blocks_all
    ).reshape(-1, head_dim)
    query_ends = jnp.concatenate([query_blocks[0], query_blocks[-1]], axis=0)
    grad_ends = jnp.concatenate([grad_blocks[0], grad_blocks[-1]], axis=0)
    end_query, end_key, end_value = attend_back(
        query_ends[None], key_rows[None], value_rows[None], grad_ends[None], log_ends, scaling
    )
    grad_query = jnp.concatenate(
        [end_query[:, :BLOCK], mid_query, end_query[:, BLOCK:]], axis=0
    ).reshape(-1, head_dim)
    return (
        grad_query.astype(jnp.bfloat16),
        (key_sum + end_key[0]).astype(jnp.bfloat16),
        (value_sum + end_value[0]).astype(jnp.bfloat16),
    )


def factored(weight, gradient, row_sum, col_sum, whole_sum, row_total, col_total):
    row_mean = row_sum / col_total + EPS_FACTOR
    col_mean = col_sum / row_total + EPS_FACTOR
    whole = whole_sum / (row_total * col_total) + EPS_FACTOR
    row_factor = row_mean / whole[..., None]
    col_factor = col_mean / whole[..., None]
    update = gradient * lax.rsqrt(
        row_factor[..., :, None] * col_factor[..., None, :] * whole[..., None, None]
    )
    return (weight - LEARN_RATE * update, row_factor, col_factor)


def body(
    tokens,
    cotangent,
    w_qkv,
    w_out,
    w_up,
    w_down,
    gain_attn,
    shift_attn,
    gain_ffn,
    shift_ffn,
    bias_up,
    bias_down,
    random_blocks,
):
    qkv_low, out_low, up_low, down_low = (
        lax.all_gather(w_qkv.astype(jnp.bfloat16), "dp", axis=1, tiled=True),
        lax.all_gather(w_out.astype(jnp.bfloat16), "dp", axis=1, tiled=True),
        lax.all_gather(w_up.astype(jnp.bfloat16), "dp", axis=0, tiled=True),
        lax.all_gather(w_down.astype(jnp.bfloat16), "dp", axis=1, tiled=True),
    )
    local_heads = random_blocks.shape[1]
    head_dim = qkv_low.shape[2] // local_heads
    inputs = tokens[0].astype(jnp.float32)
    normed_low, normal_one, inverse_one = norm_forward(inputs, gain_attn, shift_attn)
    normed_full = spread_rows(normed_low)
    seq_rows = normed_full.shape[0]
    blocks_all = seq_rows // BLOCK
    tables = jax.vmap(lambda random_rows: block_table(random_rows, blocks_all))(random_blocks[0])
    project = jnp.einsum(
        "ld,cde->cle", normed_full, qkv_low, preferred_element_type=jnp.float32
    ).astype(jnp.bfloat16)
    heads_split = project.reshape(3, seq_rows, local_heads, head_dim).transpose(0, 2, 1, 3)
    attended, log_mid, log_ends = lax.map(
        lambda members: head_forward(*members),
        (heads_split[0], heads_split[1], heads_split[2], tables),
    )
    heads_out = attended.transpose(1, 0, 2).reshape(seq_rows, local_heads * head_dim)
    branch_part = jnp.dot(heads_out, out_low, preferred_element_type=jnp.float32)
    middle = inputs + combine_heads(branch_part)
    second_low, normal_two, inverse_two = norm_forward(middle, gain_ffn, shift_ffn)
    second_full = spread_rows(second_low)
    hidden_pre = jnp.dot(second_full, up_low, preferred_element_type=jnp.float32) + bias_up
    activated, gelu_pull = jax.vjp(gelu_tanh, hidden_pre)
    active_low = activated.astype(jnp.bfloat16)
    ffn_out = combine_heads(jnp.dot(active_low, down_low, preferred_element_type=jnp.float32))
    out_tokens = (middle + ffn_out + bias_down).astype(jnp.bfloat16)
    grad_top = cotangent[0]
    grad_top_full = spread_grads(grad_top)
    grad_down_w = jnp.einsum(
        "lf,ld->fd", active_low, grad_top_full, preferred_element_type=jnp.float32
    )
    grad_active = jnp.einsum(
        "ld,fd->lf", grad_top_full, down_low, preferred_element_type=jnp.float32
    )
    grad_hidden = gelu_pull(grad_active)[0].astype(jnp.bfloat16)
    grad_bias_up = jnp.sum(grad_hidden.astype(jnp.float32), axis=0)
    grad_up_w = jnp.einsum(
        "ld,lf->df", second_full, grad_hidden, preferred_element_type=jnp.float32
    )
    grad_second = combine_grads(
        jnp.einsum("lf,df->ld", grad_hidden, up_low, preferred_element_type=jnp.float32)
    )
    grad_middle_norm, grad_gain_ffn, grad_shift_ffn = norm_backward(
        grad_second, gain_ffn, normal_two, inverse_two
    )
    grad_top_float = grad_top.astype(jnp.float32)
    grad_middle = grad_top_float + grad_middle_norm
    grad_bias_down = jnp.sum(grad_top_float, axis=0)
    grad_branch_full = spread_grads(grad_middle.astype(jnp.bfloat16))
    grad_out_w = jnp.einsum(
        "la,ld->ad", heads_out, grad_branch_full, preferred_element_type=jnp.float32
    )
    grad_heads = jnp.einsum(
        "ld,ad->la", grad_branch_full, out_low, preferred_element_type=jnp.float32
    ).astype(jnp.bfloat16)
    grad_split = grad_heads.reshape(seq_rows, local_heads, head_dim).transpose(1, 0, 2)
    grad_query, grad_key, grad_value = lax.map(
        lambda members: head_backward(*members),
        (heads_split[0], heads_split[1], heads_split[2], tables, grad_split, log_mid, log_ends),
    )
    grad_project = (
        jnp.stack([grad_query, grad_key, grad_value])
        .transpose(0, 2, 1, 3)
        .reshape(3, seq_rows, local_heads * head_dim)
    )
    grad_qkv_w = jnp.einsum(
        "ld,cle->cde", normed_full, grad_project, preferred_element_type=jnp.float32
    )
    grad_normed = combine_grads(
        jnp.einsum("cle,cde->ld", grad_project, qkv_low, preferred_element_type=jnp.float32)
    )
    grad_input_norm, grad_gain_attn, grad_shift_attn = norm_backward(
        grad_normed, gain_attn, normal_one, inverse_one
    )
    grad_tokens = (grad_middle + grad_input_norm)[None]
    shard_qkv, shard_out, shard_up, shard_down = (
        lax.psum_scatter(
            grad_qkv_w.astype(jnp.bfloat16), "dp", scatter_dimension=1, tiled=True
        ).astype(jnp.float32),
        lax.psum_scatter(
            grad_out_w.astype(jnp.bfloat16), "dp", scatter_dimension=1, tiled=True
        ).astype(jnp.float32),
        lax.psum_scatter(
            grad_up_w.astype(jnp.bfloat16), "dp", scatter_dimension=0, tiled=True
        ).astype(jnp.float32),
        lax.psum_scatter(
            grad_down_w.astype(jnp.bfloat16), "dp", scatter_dimension=1, tiled=True
        ).astype(jnp.float32),
    )
    square_qkv = shard_qkv * shard_qkv
    square_out = shard_out * shard_out
    square_up = shard_up * shard_up
    square_down = shard_down * shard_down
    mp_terms = (
        jnp.sum(square_qkv, axis=2),
        jnp.sum(square_out, axis=0),
        jnp.sum(square_up, axis=1),
        jnp.sum(square_down, axis=0),
    )
    dp_terms = (
        jnp.sum(square_qkv, axis=1),
        jnp.sum(square_out, axis=1),
        jnp.sum(square_up, axis=0),
        jnp.sum(square_down, axis=1),
    )
    token_grads = (grad_gain_attn, grad_shift_attn, grad_gain_ffn, grad_shift_ffn, grad_bias_down)
    local_totals = (
        jnp.sum(square_qkv, axis=(1, 2)),
        jnp.sum(square_out),
        jnp.sum(square_up),
        jnp.sum(square_down),
    )
    mp_input = mp_terms + token_grads
    mp_sums = tuple(lax.psum(mp_input, "mp"))
    dp_input = dp_terms + mp_sums[4:9] + (grad_bias_up,)
    dp_sums = tuple(lax.psum(dp_input, "dp"))
    totals = tuple(
        lax.psum((local_totals[0], local_totals[1], local_totals[2], local_totals[3]), ("dp", "mp"))
    )
    new_qkv, qkv_rows, qkv_cols = factored(
        w_qkv, shard_qkv, mp_sums[0], dp_sums[0], totals[0], D, D
    )
    new_out, out_rows, out_cols = factored(
        w_out, shard_out, dp_sums[1], mp_sums[1], totals[1], D, D
    )
    new_up, up_rows, up_cols = factored(w_up, shard_up, mp_sums[2], dp_sums[2], totals[2], D, FF)
    new_down, down_rows, down_cols = factored(
        w_down, shard_down, dp_sums[3], mp_sums[3], totals[3], FF, D
    )
    return (
        out_tokens[None],
        grad_tokens,
        new_qkv,
        qkv_rows,
        qkv_cols,
        new_out,
        out_rows,
        out_cols,
        new_up,
        up_rows,
        up_cols,
        new_down,
        down_rows,
        down_cols,
        dp_sums[4],
        dp_sums[5],
        dp_sums[6],
        dp_sums[7],
        dp_sums[9],
        dp_sums[8],
    )


def solution(mesh):
    placed = (
        P("dp", "mp", None),
        P("dp", "mp", None),
        P(None, "dp", "mp"),
        P("mp", "dp"),
        P("dp", "mp"),
        P("mp", "dp"),
        P(),
        P(),
        P(),
        P(),
        P("mp"),
        P(),
        P("dp", "mp", None, None),
    )
    return jax.shard_map(
        body,
        mesh=mesh,
        in_specs=placed,
        out_specs=(
            P("dp", "mp", None),
            P("dp", "mp", None),
            P(None, "dp", "mp"),
            P(None, "dp"),
            P(None, "mp"),
            P("mp", "dp"),
            P("mp"),
            P("dp"),
            P("dp", "mp"),
            P("dp"),
            P("mp"),
            P("mp", "dp"),
            P("mp"),
            P("dp"),
            P(),
            P(),
            P(),
            P(),
            P("mp"),
            P(),
        ),
        check_vma=False,
    )
```

profile of v0, /device:TPU:0, one launch (start us, length us, event | category | flops | bytes accessed | tf_op | source)
XLA Modules:
  0.0 1205.3 jit_solution(2356265805523504589)
XLA Ops:
  15.6 31.7 %all_gather.26 = bf16[256,1024]{1,0:T(8,128)(2,1)S(1)} all-gather(bf16[256,128]{1,0:T(8,128)(2,1)S(1)} %convert_element_type.165), channel_id=1, replica_groups=mesh['dp'=8,'mp'=4] {'dp'}, dimensions={1}, use_global_device_ids=true | all-gather | bytes 589824 | tf_op jit(solution)/shard_map/all_gather | solution.py:193
  47.2 15.1 %all-gather.11.cloned.1.call-done = bf16[3,1024,256]{1,2,0:T(8,128)(2,1)} async-done(((bf16[3,128,256]{1,2,0:T(8,128)(2,1)}), bf16[3,1024,256]{1,2,0:T(8,128)(2,1)}) %all-gather.11.cloned.1.call-update) | async-done | bytes 1572880 | tf_op jit(solution)/shard_map/all_gather | solution.py:192
  62.3 35.4 %all-gather.9.cloned.1.call-done = bf16[2048,1024]{1,0:T(8,128)(2,1)} async-done(((bf16[512,1024]{1,0:T(8,128)(2,1)}), bf16[2048,1024]{1,0:T(8,128)(2,1)}) %all-gather.9.cloned.1.call-update) | async-done | bytes 4194320 | tf_op jit(solution)/shard_map/all_gather | solution.py:37
  97.8 7.8 fusion.54
  105.6 6.6 copy.98
  112.2 5.7 slice_bitcast_fusion
  119.0 85.0 %while.28 = (s32[]{:T(128)}, bf16[4,2048,64]{1,2,0:T(8,128)(2,1)}, f32[4,30,64,1]{2,1,3,0:T(8,128)}, f32[4,1,128,1]{2,3,1,0:T(1,128)}, bf16[4,2048,64]{2,1,0:T(8...) while((s32[]{:T(128)}, bf16[4,2048,64]{1,2,0:T(8,128)(2,1)}, ...), condition=%wide.region_7.9_spmd, body=%wide.region_2.8_spmd.sunk | while | flops 331841952 | bytes 38948568 | solution.py:209
  130.7 3.8 broadcast_select_fusion.6
  149.0 3.0 gather_fusion.1
  152.0 3.8 broadcast_select_fusion.6
  170.3 3.0 gather_fusion.1
  173.2 3.8 broadcast_select_fusion.6
  194.5 3.8 broadcast_select_fusion.6
  204.0 4.5 convolution_convert_fusion.1
  210.3 42.8 %reduce-scatter.15.cloned.1.call-done = bf16[512,1024]{1,0:T(8,128)(2,1)} async-done(((bf16[2048,1024]{1,0:T(8,128)(2,1)}), bf16[512,1024]{1,0:T(8,128)(2,1)}) %reduce-scatter.15.cloned.1.call-update) | async-done | bytes 1048592 | tf_op jit(solution)/shard_map/reduce_scatter | solution.py:45
  259.7 8.7 reduce-scatter.19.cloned.1.call-start
  268.4 36.3 %all-gather.15.cloned.1.call-done = bf16[1024,1024]{1,0:T(8,128)(2,1)} async-done(((bf16[128,1024]{1,0:T(8,128)(2,1)}), bf16[1024,1024]{1,0:T(8,128)(2,1)}) %all-gather.15.cloned.1.call-update) | async-done | bytes 2097168 | tf_op jit(solution)/shard_map/all_gather | solution.py:194
  304.7 35.1 %all-gather.13.cloned.1.call-done = bf16[2048,1024]{1,0:T(8,128)(2,1)} async-done(((bf16[512,1024]{1,0:T(8,128)(2,1)}), bf16[2048,1024]{1,0:T(8,128)(2,1)}) %all-gather.13.cloned.1.call-update) | async-done | bytes 4194320 | tf_op jit(solution)/shard_map/all_gather | solution.py:37
  339.7 10.6 fusion.121
  350.4 43.2 %all-gather.17.cloned.1.call-done = bf16[1024,1024]{1,0:T(8,128)(2,1)} async-done(((bf16[1024,128]{1,0:T(8,128)(2,1)}), bf16[1024,1024]{1,0:T(8,128)(2,1)}) %all-gather.17.cloned.1.call-update) | async-done | bytes 2097168 | tf_op jit(solution)/shard_map/all_gather | solution.py:195
  393.5 34.3 %all-gather.21.cloned.1.call-done = bf16[1,2048,1024]{2,1,0:T(8,128)(2,1)} async-done(((bf16[1,512,1024]{2,1,0:T(8,128)(2,1)}), bf16[1,2048,1024]{2,1,0:T(8,128)(2,1)}) %all-gather.21.cloned.1.call-update) | async-done | bytes 4194320 | tf_op jit(solution)/shard_map/all_gather | solution.py:41
  427.9 15.6 %convert_reduce_fusion = (f32[1024]{0:T(1024)}, bf16[2048,1024]{1,0:T(8,128)(2,1)S(1)}) fusion(bf16[1024,1024]{1,0:T(8,128)(2,1)} %all-gather.17.cloned.1.call-done, bf16[1,2048,1024]{2,1,0:T(8,128)(2,1)} %all-gather.21.cloned.1.call-done, f32[2048,1024]{1,0:T(8,128)} %fusion.121, f32[1024]{0:T(1024)S(1)} %copy-done.59), kind=kOutput, calls=%fused_computation.108 | convolution fusion | flops 4351589376 | bytes 18882560 | tf_op jit(solution)/shard_map/ld,fd->lf/dot_general | solution.py:228
  445.5 6.3 convolution_convert_fusion.2
  452.3 44.2 %reduce-scatter.19.cloned.1.call-done = bf16[512,1024]{1,0:T(8,128)(2,1)} async-done(((bf16[2048,1024]{1,0:T(8,128)(2,1)}), bf16[512,1024]{1,0:T(8,128)(2,1)}) %reduce-scatter.19.cloned.1.call-update) | async-done | bytes 1048592 | tf_op jit(solution)/shard_map/reduce_scatter | solution.py:51
  500.6 3.2 fusion.116
  503.9 10.6 fusion.85
  517.2 9.5 convolution_convert_fusion.5
  526.8 11.7 all-gather.19.cloned.1.call-done
  538.5 3.5 convolution_convert_fusion.4
  547.1 391.1 %while.29 = (s32[]{:T(128)}, bf16[4,2048,64]{1,2,0:T(8,128)(2,1)}, bf16[4,2048,64]{1,2,0:T(8,128)(2,1)}, bf16[4,2048,64]{1,2,0:T(8,128)(2,1)}, bf16[4,2048,64]{2...) while((s32[]{:T(128)}, bf16[4,2048,64]{1,2,0:T(8,128)(2,1)}, ...), condition=%wide.region_20.22_spmd, body=%wide.region_15.21_spmd.sunk | while | flops 817038464 | bytes 143667312 | solution.py:253
  563.1 3.9 broadcast_select_fusion.7
  577.0 3.7 convolution_multiply_fusion.7
  580.8 4.8 fusion.220
  585.8 25.0 %scatter_fusion.1 = f32[32,64,64]{2,1,0:T(8,128)S(1)} fusion(f32[32,64,64]{2,1,0:T(8,128)S(1)} %broadcast.323.clone.1, s32[240]{0:T(256)S(1)} %copy-done.34, f32[240,64,64]{2,1,0:T(8,128)} %bitcast.349), kind=kCustom, calls=%fused_computation.5.clone.1 | custom fusion | flops 983040 | bytes 11797440 | tf_op jit(solution)/shard_map/while/body/eval_jaxpr/scatter-add | solution.py:146
  612.1 6.6 copy.154
  618.8 24.9 %scatter_fusion = f32[32,64,64]{2,1,0:T(8,128)S(1)} fusion(f32[32,64,64]{2,1,0:T(8,128)S(1)} %broadcast.323.clone, s32[240]{0:T(256)S(1)} %copy-done.34, f32[240,64,64]{2,1,0:T(8,128)} %bitcast.350), kind=kCustom, calls=%fused_computation.4.clone.1 | custom fusion | flops 983040 | bytes 11797440 | tf_op jit(solution)/shard_map/while/body/eval_jaxpr/scatter-add | solution.py:143
  661.0 3.8 broadcast_select_fusion.7
  674.9 3.7 convolution_multiply_fusion.7
  678.7 4.8 fusion.220
  683.6 24.9 %scatter_fusion.1 = f32[32,64,64]{2,1,0:T(8,128)S(1)} fusion(f32[32,64,64]{2,1,0:T(8,128)S(1)} %broadcast.323.clone.1, s32[240]{0:T(256)S(1)} %copy-done.34, f32[240,64,64]{2,1,0:T(8,128)} %bitcast.349), kind=kCustom, calls=%fused_computation.5.clone.1 | custom fusion | flops 983040 | bytes 11797440 | tf_op jit(solution)/shard_map/while/body/eval_jaxpr/scatter-add | solution.py:146
  709.8 6.6 copy.154
  716.6 24.9 %scatter_fusion = f32[32,64,64]{2,1,0:T(8,128)S(1)} fusion(f32[32,64,64]{2,1,0:T(8,128)S(1)} %broadcast.323.clone, s32[240]{0:T(256)S(1)} %copy-done.34, f32[240,64,64]{2,1,0:T(8,128)} %bitcast.350), kind=kCustom, calls=%fused_computation.4.clone.1 | custom fusion | flops 983040 | bytes 11797440 | tf_op jit(solution)/shard_map/while/body/eval_jaxpr/scatter-add | solution.py:143
  758.7 3.8 broadcast_select_fusion.7
  772.6 3.7 convolution_multiply_fusion.7
  776.3 4.8 fusion.220
  781.3 24.9 %scatter_fusion.1 = f32[32,64,64]{2,1,0:T(8,128)S(1)} fusion(f32[32,64,64]{2,1,0:T(8,128)S(1)} %broadcast.323.clone.1, s32[240]{0:T(256)S(1)} %copy-done.34, f32[240,64,64]{2,1,0:T(8,128)} %bitcast.349), kind=kCustom, calls=%fused_computation.5.clone.1 | custom fusion | flops 983040 | bytes 11797440 | tf_op jit(solution)/shard_map/while/body/eval_jaxpr/scatter-add | solution.py:146
  807.5 6.6 copy.154
  814.2 24.9 %scatter_fusion = f32[32,64,64]{2,1,0:T(8,128)S(1)} fusion(f32[32,64,64]{2,1,0:T(8,128)S(1)} %broadcast.323.clone, s32[240]{0:T(256)S(1)} %copy-done.34, f32[240,64,64]{2,1,0:T(8,128)} %bitcast.350), kind=kCustom, calls=%fused_computation.4.clone.1 | custom fusion | flops 983040 | bytes 11797440 | tf_op jit(solution)/shard_map/while/body/eval_jaxpr/scatter-add | solution.py:143
  856.3 3.8 broadcast_select_fusion.7
  870.2 3.7 convolution_multiply_fusion.7
  874.0 4.8 fusion.220
  879.0 24.9 %scatter_fusion.1 = f32[32,64,64]{2,1,0:T(8,128)S(1)} fusion(f32[32,64,64]{2,1,0:T(8,128)S(1)} %broadcast.323.clone.1, s32[240]{0:T(256)S(1)} %copy-done.34, f32[240,64,64]{2,1,0:T(8,128)} %bitcast.349), kind=kCustom, calls=%fused_computation.5.clone.1 | custom fusion | flops 983040 | bytes 11797440 | tf_op jit(solution)/shard_map/while/body/eval_jaxpr/scatter-add | solution.py:146
  905.1 6.6 copy.154
  911.9 24.9 %scatter_fusion = f32[32,64,64]{2,1,0:T(8,128)S(1)} fusion(f32[32,64,64]{2,1,0:T(8,128)S(1)} %broadcast.323.clone, s32[240]{0:T(256)S(1)} %copy-done.34, f32[240,64,64]{2,1,0:T(8,128)} %bitcast.350), kind=kCustom, calls=%fused_computation.4.clone.1 | custom fusion | flops 983040 | bytes 11797440 | tf_op jit(solution)/shard_map/while/body/eval_jaxpr/scatter-add | solution.py:143
  938.3 4.7 convolution_convert_fusion.6
  948.4 4.5 fusion.92
  957.5 7.8 bitcast_convert_fusion
  966.8 11.1 convolution_convert_fusion.3
  983.7 23.4 %reduce-scatter.27.cloned.1.call-done = bf16[128,256]{1,0:T(8,128)(2,1)} async-done(((bf16[1024,256]{1,0:T(8,128)(2,1)}), bf16[128,256]{1,0:T(8,128)(2,1)}) %reduce-scatter.27.cloned.1.call-update) | async-done | bytes 65552
  1008.7 66.7 %reduce-scatter.25.cloned.1.call-done = bf16[128,768]{1,0:T(8,128)(2,1)} async-done(((bf16[1024,768]{1,0:T(8,128)(2,1)}), bf16[128,768]{1,0:T(8,128)(2,1)}) %reduce-scatter.25.cloned.1.call-update) | async-done | bytes 196624
  1080.8 40.3 %all-reduce = (f32[3]{0:T(128)}, f32[]{:T(128)}, f32[]{:T(128)}, f32[]{:T(128)}) all-reduce(f32[3]{0:T(128)} %get-tuple-element.246, f32[]{:T(128)} %get-tuple-element.249, f32[]{:T(128)} %get-tuple-element.243, f32[]{:T(128)} %get-tuple-element.240), channel_id=1, replica_groups=mesh['dp'=8,'mp'=4] {'dp','mp'}, use_global_device_ids=true, to_apply=%region_28.30 | all-reduce | flops 6 | bytes 48 | tf_op jit(solution)/shard_map/psum | solution.py:314
  1127.1 11.7 all-reduce.2
  1138.8 37.6 %all-reduce.1 = (f32[3,256]{1,0:T(4,128)}, f32[256]{0:T(256)}, f32[1024]{0:T(1024)}, f32[1024]{0:T(1024)}, f32[1024]{0:T(1024)}, /*index=5*/f32[1024]{0:T(1024)}...) all-reduce(f32[3,256]{1,0:T(4,128)} %get-tuple-element.247, ...), channel_id=1, replica_groups=mesh['dp'=8,'mp'=4] {'dp'}, use_global_device_ids=true, to_apply=%region_30.32 | all-reduce | flops 9216 | bytes 73728 | tf_op jit(solution)/shard_map/psum | solution.py:312
  1193.7 4.6 fusion.76
  (532 shorter events, 256.0 us)
Async XLA Ops:
  7.2 7.5 copy-start.50
  7.2 8.4 copy-start.33
  7.2 55.1 %all-gather.11.cloned.1.call-start = ((), (), s32[]{:S(2)}) async-start(), calls=%async_computation.9 | async-start | bytes 1769472 | tf_op jit(solution)/shard_map/all_gather | solution.py:192
  8.5 97.1 %copy-start.22 = (f32[3,128,256]{1,2,0:T(8,128)}, f32[3,128,256]{1,2,0:T(8,128)S(1)}, u32[]{:S(2)}) copy-start(f32[3,128,256]{1,2,0:T(8,128)S(1)} %copy.97) | copy-start | bytes 1179652
  9.3 88.5 %all-gather.9.cloned.1.call-start = ((), (), s32[]{:S(2)}) async-start(), calls=%async_computation.8 | async-start | bytes 5242880 | tf_op jit(solution)/shard_map/all_gather | solution.py:37
  14.6 238.5 %reduce-scatter.15.cloned.1.call-start = ((), (), s32[]{:S(2)}) async-start(), calls=%async_computation.10 | async-start | bytes 5242880 | tf_op jit(solution)/shard_map/reduce_scatter | solution.py:45
  47.2 156.7 %copy-start.26 = (bf16[256,1024]{1,0:T(8,128)(2,1)}, bf16[256,1024]{1,0:T(8,128)(2,1)S(1)}, u32[]{:S(2)}) copy-start(bf16[256,1024]{1,0:T(8,128)(2,1)S(1)} %all_gather.26) | copy-start | bytes 1572868
  208.4 48.1 %copy-start.37 = (f32[1024]{0:T(1024)S(1)}, f32[1024]{0:T(1024)}, u32[]{:S(2)}) copy-start(f32[1024]{0:T(1024)} %param.27) | copy-start | bytes 12292
  208.4 48.1 %copy-start.51 = (f32[1024]{0:T(1024)S(1)}, f32[1024]{0:T(1024)}, u32[]{:S(2)}) copy-start(f32[1024]{0:T(1024)} %param.28) | copy-start | bytes 12292
  208.5 96.2 %all-gather.15.cloned.1.call-start = ((), (), s32[]{:S(2)}) async-start(), calls=%async_computation.12 | async-start | bytes 2359296 | tf_op jit(solution)/shard_map/all_gather | solution.py:194
  210.2 47.9 %copy-start.28 = (f32[1024,128]{1,0:T(8,128)S(1)}, f32[1024,128]{1,0:T(8,128)}, u32[]{:S(2)}) copy-start(f32[1024,128]{1,0:T(8,128)} %param.24) | copy-start | bytes 1572868
  210.3 129.5 %all-gather.13.cloned.1.call-start = ((), (), s32[]{:S(2)}) async-start(), calls=%async_computation.11 | async-start | bytes 5242880 | tf_op jit(solution)/shard_map/all_gather | solution.py:37
  254.8 244.6 %copy-start.35 = (f32[512]{0:T(512)}, f32[512]{0:T(512)S(1)}, u32[]{:S(2)}) copy-start(f32[512]{0:T(512)S(1)} %broadcast_multiply_fusion.4) | copy-start | bytes 6148
  256.6 242.8 %copy-start.39 = (f32[512]{0:T(512)}, f32[512]{0:T(512)S(1)}, u32[]{:S(2)}) copy-start(f32[512]{0:T(512)S(1)} %add_rsqrt_fusion) | copy-start | bytes 6148
  258.1 135.4 %all-gather.17.cloned.1.call-start = ((), (), s32[]{:S(2)}) async-start(), calls=%async_computation.13 | async-start | bytes 2359296 | tf_op jit(solution)/shard_map/all_gather | solution.py:195
  258.9 168.9 %all-gather.21.cloned.1.call-start = ((), (), s32[]{:S(2)}) async-start(), calls=%async_computation.19 | async-start | bytes 5242880 | tf_op jit(solution)/shard_map/all_gather | solution.py:41
  259.7 168.2 %copy-start.59 = (f32[1024]{0:T(1024)S(1)}, f32[1024]{0:T(1024)}, u32[]{:S(2)}) copy-start(f32[1024]{0:T(1024)} %param.29) | copy-start | bytes 12292
  259.7 236.8 %reduce-scatter.19.cloned.1.call-start = ((), (), s32[]{:S(2)}) async-start(), calls=%async_computation.15 | async-start | bytes 5242880 | tf_op jit(solution)/shard_map/reduce_scatter | solution.py:51
  427.9 17.7 %copy-start.58 = (bf16[1024,1024]{1,0:T(8,128)(2,1)S(1)}, bf16[1024,1024]{1,0:T(8,128)(2,1)}, u32[]{:S(2)}) copy-start(bf16[1024,1024]{1,0:T(8,128)(2,1)} %all-gather.15.cloned.1.call-done) | copy-start | bytes 6291460
  451.8 48.8 %copy-start.9 = (bf16[1,512,1024]{2,1,0:T(8,128)(2,1)S(1)}, bf16[1,512,1024]{2,1,0:T(8,128)(2,1)}, u32[]{:S(2)}) copy-start(bf16[1,512,1024]{2,1,0:T(8,128)(2,1)} %param.20) | copy-start | bytes 3145732
  451.8 86.7 %all-gather.19.cloned.1.call-start = ((), (), s32[]{:S(2)}) async-start(), calls=%async_computation.16 | async-start | bytes 5242880 | tf_op jit(solution)/shard_map/all_gather | solution.py:41
  503.8 476.1 %reduce-scatter.29.cloned.1.call-start = ((), (), s32[]{:S(2)}) async-start(), calls=%async_computation.22 | async-start | bytes 2359296
  517.1 464.8 %reduce-scatter.23.cloned.1.call-start = ((), (), s32[]{:S(2)}) async-start(), calls=%async_computation.18 | async-start | bytes 2359296 | tf_op jit(solution)/shard_map/reduce_scatter | solution.py:279
  517.2 21.3 %copy-start.27 = (bf16[256,1024]{1,0:T(8,128)(2,1)S(1)}, bf16[256,1024]{1,0:T(8,128)(2,1)}, u32[]{:S(2)}) copy-start(bf16[256,1024]{1,0:T(8,128)(2,1)} %copy-done.26) | copy-start | bytes 1572868
  526.7 480.4 %reduce-scatter.27.cloned.1.call-start = ((), (), s32[]{:S(2)}) async-start(), calls=%async_computation.21 | async-start | bytes 589824
  552.8 15.6 %copy-start.2 = (bf16[1,1920,64]{2,1,0:T(8,128)(2,1)}, bf16[1,1920,64]{2,1,0:T(8,128)(2,1)S(1)}, u32[]{:S(2)}) copy-start(bf16[1,1920,64]{2,1,0:T(8,128)(2,1)S(1)} %get-tuple-element.530) | copy-start | bytes 737284 | tf_op jit(solution)/shard_map/while
  585.7 25.3 %copy-start.19 = (bf16[64,64]{1,0:T(8,128)(2,1)S(1)}, bf16[64,64]{1,0:T(8,128)(2,1)}, u32[]{:S(2)}) copy-start(bf16[64,64]{1,0:T(8,128)(2,1)} %copy-done.18) | copy-start | bytes 24580 | tf_op jit(solution)/shard_map/while
  585.7 25.3 %copy-start.21 = (bf16[64,64]{1,0:T(8,128)(2,1)S(1)}, bf16[64,64]{1,0:T(8,128)(2,1)}, u32[]{:S(2)}) copy-start(bf16[64,64]{1,0:T(8,128)(2,1)} %copy-done.20) | copy-start | bytes 24580 | tf_op jit(solution)/shard_map/while
  618.8 25.3 %copy-start.15 = (bf16[64,64]{1,0:T(8,128)(2,1)S(1)}, bf16[64,64]{1,0:T(8,128)(2,1)}, u32[]{:S(2)}) copy-start(bf16[64,64]{1,0:T(8,128)(2,1)} %copy-done.14) | copy-start | bytes 24580 | tf_op jit(solution)/shard_map/while
  618.8 25.3 %copy-start.17 = (bf16[64,64]{1,0:T(8,128)(2,1)S(1)}, bf16[64,64]{1,0:T(8,128)(2,1)}, u32[]{:S(2)}) copy-start(bf16[64,64]{1,0:T(8,128)(2,1)} %copy-done.16) | copy-start | bytes 24580 | tf_op jit(solution)/shard_map/while
  650.8 15.5 %copy-start.2 = (bf16[1,1920,64]{2,1,0:T(8,128)(2,1)}, bf16[1,1920,64]{2,1,0:T(8,128)(2,1)S(1)}, u32[]{:S(2)}) copy-start(bf16[1,1920,64]{2,1,0:T(8,128)(2,1)S(1)} %get-tuple-element.530) | copy-start | bytes 737284 | tf_op jit(solution)/shard_map/while
  683.6 25.2 %copy-start.19 = (bf16[64,64]{1,0:T(8,128)(2,1)S(1)}, bf16[64,64]{1,0:T(8,128)(2,1)}, u32[]{:S(2)}) copy-start(bf16[64,64]{1,0:T(8,128)(2,1)} %copy-done.18) | copy-start | bytes 24580 | tf_op jit(solution)/shard_map/while
  683.6 25.2 %copy-start.21 = (bf16[64,64]{1,0:T(8,128)(2,1)S(1)}, bf16[64,64]{1,0:T(8,128)(2,1)}, u32[]{:S(2)}) copy-start(bf16[64,64]{1,0:T(8,128)(2,1)} %copy-done.20) | copy-start | bytes 24580 | tf_op jit(solution)/shard_map/while
  716.6 25.2 %copy-start.15 = (bf16[64,64]{1,0:T(8,128)(2,1)S(1)}, bf16[64,64]{1,0:T(8,128)(2,1)}, u32[]{:S(2)}) copy-start(bf16[64,64]{1,0:T(8,128)(2,1)} %copy-done.14) | copy-start | bytes 24580 | tf_op jit(solution)/shard_map/while
  716.6 25.2 %copy-start.17 = (bf16[64,64]{1,0:T(8,128)(2,1)S(1)}, bf16[64,64]{1,0:T(8,128)(2,1)}, u32[]{:S(2)}) copy-start(bf16[64,64]{1,0:T(8,128)(2,1)} %copy-done.16) | copy-start | bytes 24580 | tf_op jit(solution)/shard_map/while
  748.5 15.5 %copy-start.2 = (bf16[1,1920,64]{2,1,0:T(8,128)(2,1)}, bf16[1,1920,64]{2,1,0:T(8,128)(2,1)S(1)}, u32[]{:S(2)}) copy-start(bf16[1,1920,64]{2,1,0:T(8,128)(2,1)S(1)} %get-tuple-element.530) | copy-start | bytes 737284 | tf_op jit(solution)/shard_map/while
  781.3 25.2 %copy-start.19 = (bf16[64,64]{1,0:T(8,128)(2,1)S(1)}, bf16[64,64]{1,0:T(8,128)(2,1)}, u32[]{:S(2)}) copy-start(bf16[64,64]{1,0:T(8,128)(2,1)} %copy-done.18) | copy-start | bytes 24580 | tf_op jit(solution)/shard_map/while
  781.3 25.2 %copy-start.21 = (bf16[64,64]{1,0:T(8,128)(2,1)S(1)}, bf16[64,64]{1,0:T(8,128)(2,1)}, u32[]{:S(2)}) copy-start(bf16[64,64]{1,0:T(8,128)(2,1)} %copy-done.20) | copy-start | bytes 24580 | tf_op jit(solution)/shard_map/while
  814.2 25.2 %copy-start.15 = (bf16[64,64]{1,0:T(8,128)(2,1)S(1)}, bf16[64,64]{1,0:T(8,128)(2,1)}, u32[]{:S(2)}) copy-start(bf16[64,64]{1,0:T(8,128)(2,1)} %copy-done.14) | copy-start | bytes 24580 | tf_op jit(solution)/shard_map/while
  814.2 25.2 %copy-start.17 = (bf16[64,64]{1,0:T(8,128)(2,1)S(1)}, bf16[64,64]{1,0:T(8,128)(2,1)}, u32[]{:S(2)}) copy-start(bf16[64,64]{1,0:T(8,128)(2,1)} %copy-done.16) | copy-start | bytes 24580 | tf_op jit(solution)/shard_map/while
  846.1 15.5 %copy-start.2 = (bf16[1,1920,64]{2,1,0:T(8,128)(2,1)}, bf16[1,1920,64]{2,1,0:T(8,128)(2,1)S(1)}, u32[]{:S(2)}) copy-start(bf16[1,1920,64]{2,1,0:T(8,128)(2,1)S(1)} %get-tuple-element.530) | copy-start | bytes 737284 | tf_op jit(solution)/shard_map/while
  878.9 25.2 %copy-start.19 = (bf16[64,64]{1,0:T(8,128)(2,1)S(1)}, bf16[64,64]{1,0:T(8,128)(2,1)}, u32[]{:S(2)}) copy-start(bf16[64,64]{1,0:T(8,128)(2,1)} %copy-done.18) | copy-start | bytes 24580 | tf_op jit(solution)/shard_map/while
  878.9 25.2 %copy-start.21 = (bf16[64,64]{1,0:T(8,128)(2,1)S(1)}, bf16[64,64]{1,0:T(8,128)(2,1)}, u32[]{:S(2)}) copy-start(bf16[64,64]{1,0:T(8,128)(2,1)} %copy-done.20) | copy-start | bytes 24580 | tf_op jit(solution)/shard_map/while
  911.9 25.2 %copy-start.15 = (bf16[64,64]{1,0:T(8,128)(2,1)S(1)}, bf16[64,64]{1,0:T(8,128)(2,1)}, u32[]{:S(2)}) copy-start(bf16[64,64]{1,0:T(8,128)(2,1)} %copy-done.14) | copy-start | bytes 24580 | tf_op jit(solution)/shard_map/while
  911.9 25.2 %copy-start.17 = (bf16[64,64]{1,0:T(8,128)(2,1)S(1)}, bf16[64,64]{1,0:T(8,128)(2,1)}, u32[]{:S(2)}) copy-start(bf16[64,64]{1,0:T(8,128)(2,1)} %copy-done.16) | copy-start | bytes 24580 | tf_op jit(solution)/shard_map/while
  938.3 6.9 copy-start.11
  945.1 130.3 %reduce-scatter.25.cloned.1.call-start = ((), (), s32[]{:S(2)}) async-start(), calls=%async_computation.20 | async-start | bytes 1769472
  957.4 166.9 %reduce-scatter.21.cloned.1.call-start = ((), (), s32[]{:S(2)}) async-start(), calls=%async_computation.17 | async-start | bytes 5242880 | tf_op jit(solution)/shard_map/reduce_scatter | solution.py:51
  965.3 228.4 %reduce-scatter.17.cloned.1.call-start = ((), (), s32[]{:S(2)}) async-start(), calls=%async_computation.14 | async-start | bytes 5242880 | tf_op jit(solution)/shard_map/reduce_scatter | solution.py:45
  978.0 146.3 %copy-start.6 = (bf16[1,512,1024]{2,1,0:T(8,128)(2,1)S(1)}, bf16[1,512,1024]{2,1,0:T(8,128)(2,1)}, u32[]{:S(2)}) copy-start(bf16[1,512,1024]{2,1,0:T(8,128)(2,1)} %param.19) | copy-start | bytes 3145732
  978.0 146.3 %copy-start.42 = (f32[512]{0:T(512)S(1)}, f32[512]{0:T(512)}, u32[]{:S(2)}) copy-start(f32[512]{0:T(512)} %copy-done.41) | copy-start | bytes 6148
  978.0 200.6 %copy-start.23 = (f32[3,128,256]{1,2,0:T(8,128)S(1)}, f32[3,128,256]{1,2,0:T(8,128)}, u32[]{:S(2)}) copy-start(f32[3,128,256]{1,2,0:T(8,128)} %copy-done.22) | copy-start | bytes 1179652
  981.1 94.3 %copy-start.25 = (bf16[1024,128]{1,0:T(8,128)(2,1)}, bf16[1024,128]{1,0:T(8,128)(2,1)S(1)}, u32[]{:S(2)}) copy-start(bf16[1024,128]{1,0:T(8,128)(2,1)S(1)} %copy.129) | copy-start | bytes 786436
  1008.0 67.4 %copy-start.32 = (bf16[256,128]{1,0:T(8,128)(2,1)}, bf16[256,128]{1,0:T(8,128)(2,1)S(1)}, u32[]{:S(2)}) copy-start(bf16[256,128]{1,0:T(8,128)(2,1)S(1)} %copy.127) | copy-start | bytes 196612
  1077.1 116.5 %copy-start.8 = (bf16[512,1024]{1,0:T(8,128)(2,1)S(1)}, bf16[512,1024]{1,0:T(8,128)(2,1)}, u32[]{:S(2)}) copy-start(bf16[512,1024]{1,0:T(8,128)(2,1)} %reduce-scatter.15.cloned.1.call-done) | copy-start | bytes 3145732
  1077.1 116.5 %copy-start.36 = (f32[512]{0:T(512)S(1)}, f32[512]{0:T(512)}, u32[]{:S(2)}) copy-start(f32[512]{0:T(512)} %copy-done.35) | copy-start | bytes 6148
  1077.1 116.5 %copy-start.38 = (f32[1024]{0:T(1024)S(1)}, f32[1024]{0:T(1024)}, u32[]{:S(2)}) copy-start(f32[1024]{0:T(1024)} %param.27) | copy-start | bytes 12292
  1077.1 116.5 %copy-start.40 = (f32[512]{0:T(512)S(1)}, f32[512]{0:T(512)}, u32[]{:S(2)}) copy-start(f32[512]{0:T(512)} %copy-done.39) | copy-start | bytes 6148
  1183.0 15.3 %copy-start.53 = (f32[128]{0:T(128)}, f32[128]{0:T(128)S(1)}, u32[]{:S(2)}) copy-start(f32[128]{0:T(128)S(1)} %add_divide_fusion.7) | copy-start | bytes 1540
  1183.7 14.7 %copy-start.54 = (f32[128]{0:T(128)}, f32[128]{0:T(128)S(1)}, u32[]{:S(2)}) copy-start(f32[128]{0:T(128)S(1)} %add_divide_fusion.6) | copy-start | bytes 1540
  1184.3 14.0 %copy-start.55 = (f32[128]{0:T(128)}, f32[128]{0:T(128)S(1)}, u32[]{:S(2)}) copy-start(f32[128]{0:T(128)S(1)} %add_divide_fusion.5) | copy-start | bytes 1540
  1185.0 13.3 %copy-start.52 = (f32[256]{0:T(256)}, f32[256]{0:T(256)S(1)}, u32[]{:S(2)}) copy-start(f32[256]{0:T(256)S(1)} %add_divide_fusion.4) | copy-start | bytes 3076
  1187.1 11.3 copy-start.47
  1187.8 10.6 copy-start.48
  (61 other events, 207.4 us)
Sparse Core Ops, SparseCore 0:
  10.7 51.6 all-gather.10
  64.5 33.2 all-gather.8
  208.6 44.5 reduce-scatter.14
  255.3 49.2 all-gather.14
  306.7 32.9 all-gather.12
  342.4 51.0 all-gather.16
  395.1 32.6 all-gather.20
  451.9 44.4 reduce-scatter.18
  504.0 34.4 all-gather.18
  541.9 67.8 reduce-scatter.28
  613.3 66.8 reduce-scatter.22
  945.2 61.8 reduce-scatter.26
  1011.5 63.8 reduce-scatter.24
  1077.8 43.9 reduce-scatter.20
  1124.4 44.6 reduce-scatter.16
where the time goes:
time: 1220 us; the launch traced here: 1210 us
  waiting for transfers between devices  389 us (32%)
  other arithmetic  303 us (25%)
  local copies, waits for them, and re-layouts  189 us (15%)
  matrix products  175 us (14%)
  blocking collectives  121 us (10%)
  between operations  16.9 us (1%)
    scatter-add x4, other arithmetic, head_backward(): jax.ops.segment_sum(mid_value.reshape(-1, BLOCK, head_dim), segment_ids,...  99.5 us
    scatter-add x4, other arithmetic, head_backward(): jax.ops.segment_sum(mid_key.reshape(-1, BLOCK, head_dim), segment_ids, nu...  99.5 us
    unnamed x18, waiting for transfers between devices  91 us
    all_gather x2, waiting for transfers between devices, spread_rows(): return lax.all_gather(local_part, 'mp', axis=0, tiled=True)  70.5 us
    gather x16, local copies, waits for them, and re-layouts, near_blocks(): jnp.take(block_rows, key_table, axis=0)  47.5 us
    all_gather x2, waiting for transfers between devices, spread_grads(): return lax.all_gather(local_part, 'mp', axis=0, tiled=True)  46 us
    reduce_scatter x2, waiting for transfers between devices, combine_grads(): lax.psum_scatter(partial_value.astype(jnp.bfloat16), 'mp', scatter_dimens...  44.2 us
    all_gather x1, waiting for transfers between devices, body(): lax.all_gather(w_down.astype(jnp.bfloat16), 'dp', axis=1, tiled=True)  43.2 us
  transfers between devices with their start and end apart: 15, of which 11 were waited for; matrix products, arithmetic and copies ran while one was open for 42% of the time, Pallas kernels for 0%

commit v1 on v0

--- a/solution.py
+++ b/solution.py
@@ -10,6 +10,28 @@
 EPS_FACTOR = 1e-30
 LEARN_RATE = 0.1
 GELU_SCALE = 0.7978845608028654
+
+
+def joined_along(blocks, dim):
+    blocks = jnp.moveaxis(blocks, 0, dim)
+    shape = blocks.shape
+    return blocks.reshape(*shape[:dim], shape[dim] * shape[dim + 1], *shape[dim + 2 :])
+
+
+def gather_around(x, axis, dim):
+    length = lax.axis_size(axis)
+    pairs = [(i, (i + 1) % length) for i in range(length)]
+    back = [(b, a) for a, b in pairs]
+    lower, upper = ([], [])
+    for step in range(length - 1):
+        if step % 2 == 0:
+            lower.append(lax.ppermute(lower[-1] if lower else x, axis, pairs))
+        else:
+            upper.append(lax.ppermute(upper[-1] if upper else x, axis, back))
+    blocks = jnp.stack([*lower[::-1], x, *upper])
+    shift = lax.axis_index(axis) - len(lower)
+    blocks = blocks[(jnp.arange(length) - shift) % length]
+    return joined_along(blocks, dim)
 
 
 def gelu_tanh(values):
@@ -191,7 +213,7 @@
     qkv_low, out_low, up_low, down_low = (
         lax.all_gather(w_qkv.astype(jnp.bfloat16), "dp", axis=1, tiled=True),
         lax.all_gather(w_out.astype(jnp.bfloat16), "dp", axis=1, tiled=True),
-        lax.all_gather(w_up.astype(jnp.bfloat16), "dp", axis=0, tiled=True),
+        gather_around(w_up.astype(jnp.bfloat16), "dp", 0),
         lax.all_gather(w_down.astype(jnp.bfloat16), "dp", axis=1, tiled=True),
     )
     local_heads = random_blocks.shape[1]

time: 1220 us -> 1180 us (0.967)
  waiting for transfers between devices: 389 us -> 316 us
  starting transfers between devices: 9.9 us -> 27.6 us
    all_gather x1 -> x0, waiting for transfers between devices: 36.3 us -> none  [body(): lax.all_gather(w_up.astype(jnp.bfloat16), 'dp', axis=0, tiled=True)]
    all_gather x2, waiting for transfers between devices: 70.5 us -> 35.4 us  [spread_rows(): return lax.all_gather(local_part, 'mp', axis=0, tiled=True)]
    ppermute x0 -> x7, starting transfers between devices: none -> 26.2 us  [the longest x3 19.6 us: gather_around(): upper.append(lax.ppermute(upper[-1] if upper else x, axis, back))]
    all_gather x1, waiting for transfers between devices: 43.2 us -> 17.4 us  [body(): lax.all_gather(w_down.astype(jnp.bfloat16), 'dp', axis=1, tiled=True)]
    ppermute x0 -> x7, waiting for transfers between devices: none -> 23 us  [the longest x4 23 us: gather_around(): lower.append(lax.ppermute(lower[-1] if lower else x, axis, pairs))]
    unnamed x103 -> x109, local copies, waits for them, and re-layouts: 28.1 us -> 33.3 us
    unnamed x18 -> x17, waiting for transfers between devices: 91 us -> 90.6 us
  transfers between devices with their start and end apart: 15 -> 21, of which waited for: 11 -> 13; matrix products, arithmetic and copies ran while one was open for 42% -> 45% of each run, Pallas kernels for 0% -> 0%
where the time goes in v1:
time: 1180 us; the launch traced here: 1160 us
  waiting for transfers between devices  316 us (27%)
  other arithmetic  303 us (26%)
  local copies, waits for them, and re-layouts  199 us (17%)
  matrix products  175 us (15%)
  blocking collectives  121 us (10%)
  starting transfers between devices  27.6 us (2%)
  between operations  16.7 us (1%)
    scatter-add x4, other arithmetic, head_backward(): jax.ops.segment_sum(mid_value.reshape(-1, BLOCK, head_dim), segment_ids,...  99.5 us
    scatter-add x4, other arithmetic, head_backward(): jax.ops.segment_sum(mid_key.reshape(-1, BLOCK, head_dim), segment_ids, nu...  99.5 us
    unnamed x17, waiting for transfers between devices  90.6 us
    gather x16, local copies, waits for them, and re-layouts, near_blocks(): jnp.take(block_rows, key_table, axis=0)  47.4 us
    all_gather x2, waiting for transfers between devices, spread_grads(): return lax.all_gather(local_part, 'mp', axis=0, tiled=True)  45.7 us
    reduce_scatter x2, waiting for transfers between devices, combine_grads(): lax.psum_scatter(partial_value.astype(jnp.bfloat16), 'mp', scatter_dimens...  44.6 us
    reduce_scatter x2, waiting for transfers between devices, combine_heads(): lax.psum_scatter(partial_value.astype(jnp.bfloat16), 'mp', scatter_dimens...  44.2 us
    psum x1, blocking collectives, body(): lax.psum((local_totals[0], local_totals[1], local_totals[2], local_totals...  40.3 us
  transfers between devices with their start and end apart: 21, of which 13 were waited for; matrix products, arithmetic and copies ran while one was open for 45% of the time, Pallas kernels for 0%

profile of v1, /device:TPU:0, one launch (start us, length us, event | category | flops | bytes accessed | tf_op | source)
XLA Modules:
  0.0 1159.9 jit_solution(3016615629254987378)
XLA Ops:
  15.6 31.7 %all_gather.23 = bf16[256,1024]{1,0:T(8,128)(2,1)S(1)} all-gather(bf16[256,128]{1,0:T(8,128)(2,1)S(1)} %convert_element_type.165), channel_id=1, replica_groups=mesh['dp'=8,'mp'=4] {'dp'}, dimensions={1}, use_global_device_ids=true | all-gather | bytes 589824 | tf_op jit(solution)/shard_map/all_gather | solution.py:215
  47.2 15.1 %all-gather.10.cloned.1.call-done = bf16[3,1024,256]{1,2,0:T(8,128)(2,1)} async-done(((bf16[3,128,256]{1,2,0:T(8,128)(2,1)}), bf16[3,1024,256]{1,2,0:T(8,128)(2,1)}) %all-gather.10.cloned.1.call-update) | async-done | bytes 1572880 | tf_op jit(solution)/shard_map/all_gather | solution.py:214
  62.4 35.4 %all-gather.8.cloned.1.call-done = bf16[2048,1024]{1,0:T(8,128)(2,1)} async-done(((bf16[512,1024]{1,0:T(8,128)(2,1)}), bf16[2048,1024]{1,0:T(8,128)(2,1)}) %all-gather.8.cloned.1.call-update) | async-done | bytes 4194320 | tf_op jit(solution)/shard_map/all_gather | solution.py:59
  97.8 7.8 fusion.54
  105.6 6.6 copy.98
  112.2 5.7 slice_bitcast_fusion
  119.0 85.0 %while.28 = (s32[]{:T(128)}, bf16[4,2048,64]{1,2,0:T(8,128)(2,1)}, f32[4,30,64,1]{2,1,3,0:T(8,128)}, f32[4,1,128,1]{2,3,1,0:T(1,128)}, bf16[4,2048,64]{2,1,0:T(8...) while((s32[]{:T(128)}, bf16[4,2048,64]{1,2,0:T(8,128)(2,1)}, ...), condition=%wide.region_7.9_spmd, body=%wide.region_2.8_spmd.sunk | while | flops 331841952 | bytes 38948568 | solution.py:231
  130.8 3.8 broadcast_select_fusion.6
  152.0 3.8 broadcast_select_fusion.6
  173.3 3.8 broadcast_select_fusion.6
  194.5 3.8 broadcast_select_fusion.6
  204.0 4.5 convolution_convert_fusion.1
  209.0 44.2 %reduce-scatter.15.cloned.1.call-done = bf16[512,1024]{1,0:T(8,128)(2,1)} async-done(((bf16[2048,1024]{1,0:T(8,128)(2,1)}), bf16[512,1024]{1,0:T(8,128)(2,1)}) %reduce-scatter.15.cloned.1.call-update) | async-done | bytes 1048592 | tf_op jit(solution)/shard_map/reduce_scatter | solution.py:67
  261.2 9.3 collective-permute-done
  270.5 4.7 collective-permute-start.4
  275.2 5.9 collective-permute-done.1
  283.6 6.7 collective-permute-start.5
  296.1 8.1 collective-permute-start.6
  304.3 4.7 collective-permute-done.3
  317.6 3.6 gather_fusion.4
  321.3 10.6 fusion.123
  331.9 17.4 %all-gather.14.cloned.1.call-done = bf16[1024,1024]{1,0:T(8,128)(2,1)} async-done(((bf16[1024,128]{1,0:T(8,128)(2,1)}), bf16[1024,1024]{1,0:T(8,128)(2,1)}) %all-gather.14.cloned.1.call-update) | async-done | bytes 2097168 | tf_op jit(solution)/shard_map/all_gather | solution.py:217
  349.3 34.2 %all-gather.18.cloned.1.call-done = bf16[1,2048,1024]{2,1,0:T(8,128)(2,1)} async-done(((bf16[1,512,1024]{2,1,0:T(8,128)(2,1)}), bf16[1,2048,1024]{2,1,0:T(8,128)(2,1)}) %all-gather.18.cloned.1.call-update) | async-done | bytes 4194320 | tf_op jit(solution)/shard_map/all_gather | solution.py:63
  383.5 15.8 %convert_reduce_fusion = (f32[1024]{0:T(1024)}, bf16[2048,1024]{1,0:T(8,128)(2,1)S(1)}) fusion(bf16[1024,1024]{1,0:T(8,128)(2,1)} %all-gather.14.cloned.1.call-done, bf16[1,2048,1024]{2,1,0:T(8,128)(2,1)} %all-gather.18.cloned.1.call-done, f32[2048,1024]{1,0:T(8,128)} %fusion.123, f32[1024]{0:T(1024)S(1)} %copy-done.59), kind=kOutput, calls=%fused_computation.109 | convolution fusion | flops 4351589376 | bytes 18882560 | tf_op jit(solution)/shard_map/ld,fd->lf/dot_general | solution.py:250
  401.2 6.3 convolution_convert_fusion.2
  407.6 44.6 %reduce-scatter.19.cloned.1.call-done = bf16[512,1024]{1,0:T(8,128)(2,1)} async-done(((bf16[2048,1024]{1,0:T(8,128)(2,1)}), bf16[512,1024]{1,0:T(8,128)(2,1)}) %reduce-scatter.19.cloned.1.call-update) | async-done | bytes 1048592 | tf_op jit(solution)/shard_map/reduce_scatter | solution.py:73
  458.7 10.6 fusion.85
  472.1 9.4 convolution_convert_fusion.5
  481.6 11.5 all-gather.16.cloned.1.call-done
  502.2 391.1 %while.29 = (s32[]{:T(128)}, bf16[4,2048,64]{1,2,0:T(8,128)(2,1)}, bf16[4,2048,64]{1,2,0:T(8,128)(2,1)}, bf16[4,2048,64]{1,2,0:T(8,128)(2,1)}, bf16[4,2048,64]{2...) while((s32[]{:T(128)}, bf16[4,2048,64]{1,2,0:T(8,128)(2,1)}, ...), condition=%wide.region_20.22_spmd, body=%wide.region_15.21_spmd.sunk | while | flops 817038464 | bytes 143667312 | solution.py:275
  518.1 3.9 broadcast_select_fusion.7
  532.1 3.7 convolution_multiply_fusion.7
  535.8 4.8 fusion.222
  540.8 25.0 %scatter_fusion.1 = f32[32,64,64]{2,1,0:T(8,128)S(1)} fusion(f32[32,64,64]{2,1,0:T(8,128)S(1)} %broadcast.392.clone.1, s32[240]{0:T(256)S(1)} %copy-done.35, f32[240,64,64]{2,1,0:T(8,128)} %bitcast.368), kind=kCustom, calls=%fused_computation.6.clone.1 | custom fusion | flops 983040 | bytes 11797440 | tf_op jit(solution)/shard_map/while/body/eval_jaxpr/scatter-add | solution.py:168
  567.1 6.6 copy.154
  573.9 24.9 %scatter_fusion = f32[32,64,64]{2,1,0:T(8,128)S(1)} fusion(f32[32,64,64]{2,1,0:T(8,128)S(1)} %broadcast.392.clone, s32[240]{0:T(256)S(1)} %copy-done.35, f32[240,64,64]{2,1,0:T(8,128)} %bitcast.369), kind=kCustom, calls=%fused_computation.5.clone.1 | custom fusion | flops 983040 | bytes 11797440 | tf_op jit(solution)/shard_map/while/body/eval_jaxpr/scatter-add | solution.py:165
  616.0 3.8 broadcast_select_fusion.7
  629.9 3.7 convolution_multiply_fusion.7
  633.7 4.8 fusion.222
  638.6 24.9 %scatter_fusion.1 = f32[32,64,64]{2,1,0:T(8,128)S(1)} fusion(f32[32,64,64]{2,1,0:T(8,128)S(1)} %broadcast.392.clone.1, s32[240]{0:T(256)S(1)} %copy-done.35, f32[240,64,64]{2,1,0:T(8,128)} %bitcast.368), kind=kCustom, calls=%fused_computation.6.clone.1 | custom fusion | flops 983040 | bytes 11797440 | tf_op jit(solution)/shard_map/while/body/eval_jaxpr/scatter-add | solution.py:168
  664.8 6.6 copy.154
  671.6 24.9 %scatter_fusion = f32[32,64,64]{2,1,0:T(8,128)S(1)} fusion(f32[32,64,64]{2,1,0:T(8,128)S(1)} %broadcast.392.clone, s32[240]{0:T(256)S(1)} %copy-done.35, f32[240,64,64]{2,1,0:T(8,128)} %bitcast.369), kind=kCustom, calls=%fused_computation.5.clone.1 | custom fusion | flops 983040 | bytes 11797440 | tf_op jit(solution)/shard_map/while/body/eval_jaxpr/scatter-add | solution.py:165
  713.7 3.8 broadcast_select_fusion.7
  727.6 3.7 convolution_multiply_fusion.7
  731.3 4.8 fusion.222
  736.3 24.9 %scatter_fusion.1 = f32[32,64,64]{2,1,0:T(8,128)S(1)} fusion(f32[32,64,64]{2,1,0:T(8,128)S(1)} %broadcast.392.clone.1, s32[240]{0:T(256)S(1)} %copy-done.35, f32[240,64,64]{2,1,0:T(8,128)} %bitcast.368), kind=kCustom, calls=%fused_computation.6.clone.1 | custom fusion | flops 983040 | bytes 11797440 | tf_op jit(solution)/shard_map/while/body/eval_jaxpr/scatter-add | solution.py:168
  762.5 6.6 copy.154
  769.3 24.9 %scatter_fusion = f32[32,64,64]{2,1,0:T(8,128)S(1)} fusion(f32[32,64,64]{2,1,0:T(8,128)S(1)} %broadcast.392.clone, s32[240]{0:T(256)S(1)} %copy-done.35, f32[240,64,64]{2,1,0:T(8,128)} %bitcast.369), kind=kCustom, calls=%fused_computation.5.clone.1 | custom fusion | flops 983040 | bytes 11797440 | tf_op jit(solution)/shard_map/while/body/eval_jaxpr/scatter-add | solution.py:165
  811.3 3.8 broadcast_select_fusion.7
  825.2 3.7 convolution_multiply_fusion.7
  829.0 4.8 fusion.222
  833.9 24.9 %scatter_fusion.1 = f32[32,64,64]{2,1,0:T(8,128)S(1)} fusion(f32[32,64,64]{2,1,0:T(8,128)S(1)} %broadcast.392.clone.1, s32[240]{0:T(256)S(1)} %copy-done.35, f32[240,64,64]{2,1,0:T(8,128)} %bitcast.368), kind=kCustom, calls=%fused_computation.6.clone.1 | custom fusion | flops 983040 | bytes 11797440 | tf_op jit(solution)/shard_map/while/body/eval_jaxpr/scatter-add | solution.py:168
  860.1 6.6 copy.154
  866.9 24.9 %scatter_fusion = f32[32,64,64]{2,1,0:T(8,128)S(1)} fusion(f32[32,64,64]{2,1,0:T(8,128)S(1)} %broadcast.392.clone, s32[240]{0:T(256)S(1)} %copy-done.35, f32[240,64,64]{2,1,0:T(8,128)} %bitcast.369), kind=kCustom, calls=%fused_computation.5.clone.1 | custom fusion | flops 983040 | bytes 11797440 | tf_op jit(solution)/shard_map/while/body/eval_jaxpr/scatter-add | solution.py:165
  893.3 4.7 convolution_convert_fusion.6
  903.4 4.5 fusion.92
  912.5 7.8 bitcast_convert_fusion
  921.8 11.1 convolution_convert_fusion.3
  938.7 23.3 %reduce-scatter.27.cloned.1.call-done = bf16[128,256]{1,0:T(8,128)(2,1)} async-done(((bf16[1024,256]{1,0:T(8,128)(2,1)}), bf16[128,256]{1,0:T(8,128)(2,1)}) %reduce-scatter.27.cloned.1.call-update) | async-done | bytes 65552
  963.7 66.5 %reduce-scatter.25.cloned.1.call-done = bf16[128,768]{1,0:T(8,128)(2,1)} async-done(((bf16[1024,768]{1,0:T(8,128)(2,1)}), bf16[128,768]{1,0:T(8,128)(2,1)}) %reduce-scatter.25.cloned.1.call-update) | async-done | bytes 196624
  1035.6 40.3 %all-reduce = (f32[3]{0:T(128)}, f32[]{:T(128)}, f32[]{:T(128)}, f32[]{:T(128)}) all-reduce(f32[3]{0:T(128)} %get-tuple-element.246, f32[]{:T(128)} %get-tuple-element.249, f32[]{:T(128)} %get-tuple-element.243, f32[]{:T(128)} %get-tuple-element.240), channel_id=1, replica_groups=mesh['dp'=8,'mp'=4] {'dp','mp'}, use_global_device_ids=true, to_apply=%region_28.30 | all-reduce | flops 6 | bytes 48 | tf_op jit(solution)/shard_map/psum | solution.py:336
  1081.9 11.8 %all-reduce.2 = (f32[1024]{0:T(1024)}, f32[1024]{0:T(1024)}, f32[1024]{0:T(1024)}, f32[1024]{0:T(1024)}, f32[1024]{0:T(1024)}, /*index=5*/f32[3,128]{1,0:T(4,128)}, f32[128]{0:T(128)}, f32[128]{0:T(128)}, f32[128]{0:T(128)}) all-reduce(f32[1024]{0:T(1024)} %get-tuple-element.233, ...), channel_id=1, replica_groups=mesh['dp'=8,'mp'=4] {'mp'}, use_global_device_ids=true, to_apply=%region_53.55 | all-reduce | flops 5888 | bytes 47104 | tf_op jit(solution)/shard_map/psum | solution.py:332
  1093.6 37.6 %all-reduce.1 = (f32[3,256]{1,0:T(4,128)}, f32[256]{0:T(256)}, f32[1024]{0:T(1024)}, f32[1024]{0:T(1024)}, f32[1024]{0:T(1024)}, /*index=5*/f32[1024]{0:T(1024)}...) all-reduce(f32[3,256]{1,0:T(4,128)} %get-tuple-element.247, ...), channel_id=1, replica_groups=mesh['dp'=8,'mp'=4] {'dp'}, use_global_device_ids=true, to_apply=%region_30.32 | all-reduce | flops 9216 | bytes 73728 | tf_op jit(solution)/shard_map/psum | solution.py:334
  1148.5 4.6 fusion.76
  (554 shorter events, 284.8 us)
Async XLA Ops:
  7.2 55.2 %all-gather.10.cloned.1.call-start = ((), (), s32[]{:S(2)}) async-start(), calls=%async_computation.9 | async-start | bytes 1769472 | tf_op jit(solution)/shard_map/all_gather | solution.py:214
  8.5 97.1 %copy-start.23 = (f32[3,128,256]{1,2,0:T(8,128)}, f32[3,128,256]{1,2,0:T(8,128)S(1)}, u32[]{:S(2)}) copy-start(f32[3,128,256]{1,2,0:T(8,128)S(1)} %copy.97) | copy-start | bytes 1179652
  9.3 88.5 %all-gather.8.cloned.1.call-start = ((), (), s32[]{:S(2)}) async-start(), calls=%async_computation.8 | async-start | bytes 5242880 | tf_op jit(solution)/shard_map/all_gather | solution.py:59
  14.6 238.6 %reduce-scatter.15.cloned.1.call-start = ((), (), s32[]{:S(2)}) async-start(), calls=%async_computation.10 | async-start | bytes 5242880 | tf_op jit(solution)/shard_map/reduce_scatter | solution.py:67
  47.2 156.8 %copy-start.27 = (bf16[256,1024]{1,0:T(8,128)(2,1)}, bf16[256,1024]{1,0:T(8,128)(2,1)S(1)}, u32[]{:S(2)}) copy-start(bf16[256,1024]{1,0:T(8,128)(2,1)S(1)} %all_gather.23) | copy-start | bytes 1572868
  208.5 48.2 %copy-start.38 = (f32[1024]{0:T(1024)S(1)}, f32[1024]{0:T(1024)}, u32[]{:S(2)}) copy-start(f32[1024]{0:T(1024)} %param.27) | copy-start | bytes 12292
  208.5 48.2 %copy-start.52 = (f32[1024]{0:T(1024)S(1)}, f32[1024]{0:T(1024)}, u32[]{:S(2)}) copy-start(f32[1024]{0:T(1024)} %param.28) | copy-start | bytes 12292
  208.5 49.8 %copy-start.30 = (f32[1024,128]{1,0:T(8,128)S(1)}, f32[1024,128]{1,0:T(8,128)}, u32[]{:S(2)}) copy-start(f32[1024,128]{1,0:T(8,128)} %param.24) | copy-start | bytes 1572868
  208.5 112.8 %all-gather.12.cloned.1.call-start = ((), (), s32[]{:S(2)}) async-start(), calls=%async_computation.11 | async-start | bytes 5242880 | tf_op jit(solution)/shard_map/all_gather | solution.py:59
  254.8 200.4 %copy-start.36 = (f32[512]{0:T(512)}, f32[512]{0:T(512)S(1)}, u32[]{:S(2)}) copy-start(f32[512]{0:T(512)S(1)} %broadcast_multiply_fusion.4) | copy-start | bytes 6148
  256.7 198.5 %copy-start.40 = (f32[512]{0:T(512)}, f32[512]{0:T(512)S(1)}, u32[]{:S(2)}) copy-start(f32[512]{0:T(512)S(1)} %add_rsqrt_fusion) | copy-start | bytes 6148
  258.2 91.1 %all-gather.14.cloned.1.call-start = ((), (), s32[]{:S(2)}) async-start(), calls=%async_computation.12 | async-start | bytes 2359296 | tf_op jit(solution)/shard_map/all_gather | solution.py:217
  259.0 124.5 %all-gather.18.cloned.1.call-start = ((), (), s32[]{:S(2)}) async-start(), calls=%async_computation.18 | async-start | bytes 5242880 | tf_op jit(solution)/shard_map/all_gather | solution.py:63
  259.6 192.6 %reduce-scatter.19.cloned.1.call-start = ((), (), s32[]{:S(2)}) async-start(), calls=%async_computation.14 | async-start | bytes 5242880 | tf_op jit(solution)/shard_map/reduce_scatter | solution.py:73
  259.7 10.8 collective-permute-start
  270.5 10.6 collective-permute-start.1
  270.5 13.1 %collective-permute-start.4 = (bf16[128,1024]{1,0:T(8,128)(2,1)S(1)}, bf16[128,1024]{1,0:T(8,128)(2,1)S(1)}, u32[]{:S(2)}, u32[]{:S(2)}) collective-permute-start(bf16[128,1024]{1,0:T(8,128)(2,1)S(1)} %convert_element_type.169), channel_id=1, source_target_pairs={{4,0},{8,4},{12,8},{16,12},{20,16},{24,20},{28,24},{0,28},{5,1},{9... | collective-permute-start | bytes 786440 | tf_op jit(solution)/shard_map/ppermute | solution.py:30
  281.1 12.4 %collective-permute-start.2 = (bf16[128,1024]{1,0:T(8,128)(2,1)S(1)}, bf16[128,1024]{1,0:T(8,128)(2,1)}, u32[]{:S(2)}, u32[]{:S(2)}) collective-permute-start(bf16[128,1024]{1,0:T(8,128)(2,1)S(1)} %collective-permute-done.1), channel_id=1, source_target_pairs={{0,4},{4,8},{8,12},{12,16},{16,20},{20,24},{24,28},{28,0},{1,5},{5... | collective-permute-start | bytes 786440 | tf_op jit(solution)/shard_map/ppermute | solution.py:28
  283.6 12.5 %collective-permute-start.5 = (bf16[128,1024]{1,0:T(8,128)(2,1)S(1)}, bf16[128,1024]{1,0:T(8,128)(2,1)}, u32[]{:S(2)}, u32[]{:S(2)}) collective-permute-start(bf16[128,1024]{1,0:T(8,128)(2,1)S(1)} %collective-permute-done.4), channel_id=1, source_target_pairs={{4,0},{8,4},{12,8},{16,12},{20,16},{24,20},{28,24},{0,28},{5,1},{9... | collective-permute-start | bytes 786440 | tf_op jit(solution)/shard_map/ppermute | solution.py:30
  293.5 15.5 %collective-permute-start.3 = (bf16[128,1024]{1,0:T(8,128)(2,1)}, bf16[128,1024]{1,0:T(8,128)(2,1)}, u32[]{:S(2)}, u32[]{:S(2)}) collective-permute-start(bf16[128,1024]{1,0:T(8,128)(2,1)} %collective-permute-done.2), channel_id=1, source_target_pairs={{0,4},{4,8},{8,12},{12,16},{16,20},{20,24},{24,28},{28,0},{1,5},{5... | collective-permute-start | bytes 786440 | tf_op jit(solution)/shard_map/ppermute | solution.py:28
  296.1 20.8 %collective-permute-start.6 = (bf16[128,1024]{1,0:T(8,128)(2,1)}, bf16[128,1024]{1,0:T(8,128)(2,1)S(1)}, u32[]{:S(2)}, u32[]{:S(2)}) collective-permute-start(bf16[128,1024]{1,0:T(8,128)(2,1)} %collective-permute-done.5), channel_id=1, source_target_pairs={{4,0},{8,4},{12,8},{16,12},{20,16},{24,20},{28,24},{0,28},{5,1},{9... | collective-permute-start | bytes 786440 | tf_op jit(solution)/shard_map/ppermute | solution.py:30
  321.3 62.3 %copy-start.59 = (f32[1024]{0:T(1024)S(1)}, f32[1024]{0:T(1024)}, u32[]{:S(2)}) copy-start(f32[1024]{0:T(1024)} %param.29) | copy-start | bytes 12292
  383.5 17.7 %copy-start.29 = (bf16[8,128,1024]{2,1,0:T(8,128)(2,1)S(1)}, bf16[8,128,1024]{2,1,0:T(8,128)(2,1)}, u32[]{:S(2)}) copy-start(bf16[8,128,1024]{2,1,0:T(8,128)(2,1)} %gather_fusion.4) | copy-start | bytes 6291460
  407.5 47.7 %copy-start.9 = (bf16[1,512,1024]{2,1,0:T(8,128)(2,1)S(1)}, bf16[1,512,1024]{2,1,0:T(8,128)(2,1)}, u32[]{:S(2)}) copy-start(bf16[1,512,1024]{2,1,0:T(8,128)(2,1)} %param.20) | copy-start | bytes 3145732
  407.6 85.6 %all-gather.16.cloned.1.call-start = ((), (), s32[]{:S(2)}) async-start(), calls=%async_computation.15 | async-start | bytes 5242880 | tf_op jit(solution)/shard_map/all_gather | solution.py:63
  455.2 14.2 %copy-start.45 = (f32[512]{0:T(512)}, f32[512]{0:T(512)S(1)}, u32[]{:S(2)}) copy-start(f32[512]{0:T(512)S(1)} %broadcast_multiply_fusion.2) | copy-start | bytes 6148
  458.5 476.5 %reduce-scatter.29.cloned.1.call-start = ((), (), s32[]{:S(2)}) async-start(), calls=%async_computation.21 | async-start | bytes 2359296
  472.1 464.9 %reduce-scatter.23.cloned.1.call-start = ((), (), s32[]{:S(2)}) async-start(), calls=%async_computation.17 | async-start | bytes 2359296 | tf_op jit(solution)/shard_map/reduce_scatter | solution.py:301
  472.1 21.0 %copy-start.28 = (bf16[256,1024]{1,0:T(8,128)(2,1)S(1)}, bf16[256,1024]{1,0:T(8,128)(2,1)}, u32[]{:S(2)}) copy-start(bf16[256,1024]{1,0:T(8,128)(2,1)} %copy-done.27) | copy-start | bytes 1572868
  481.6 480.5 %reduce-scatter.27.cloned.1.call-start = ((), (), s32[]{:S(2)}) async-start(), calls=%async_computation.20 | async-start | bytes 589824
  507.9 15.6 %copy-start.2 = (bf16[1,1920,64]{2,1,0:T(8,128)(2,1)}, bf16[1,1920,64]{2,1,0:T(8,128)(2,1)S(1)}, u32[]{:S(2)}) copy-start(bf16[1,1920,64]{2,1,0:T(8,128)(2,1)S(1)} %get-tuple-element.530) | copy-start | bytes 737284 | tf_op jit(solution)/shard_map/while
  540.8 25.3 %copy-start.20 = (bf16[64,64]{1,0:T(8,128)(2,1)S(1)}, bf16[64,64]{1,0:T(8,128)(2,1)}, u32[]{:S(2)}) copy-start(bf16[64,64]{1,0:T(8,128)(2,1)} %copy-done.19) | copy-start | bytes 24580 | tf_op jit(solution)/shard_map/while
  540.8 25.3 %copy-start.22 = (bf16[64,64]{1,0:T(8,128)(2,1)S(1)}, bf16[64,64]{1,0:T(8,128)(2,1)}, u32[]{:S(2)}) copy-start(bf16[64,64]{1,0:T(8,128)(2,1)} %copy-done.21) | copy-start | bytes 24580 | tf_op jit(solution)/shard_map/while
  573.8 25.3 %copy-start.16 = (bf16[64,64]{1,0:T(8,128)(2,1)S(1)}, bf16[64,64]{1,0:T(8,128)(2,1)}, u32[]{:S(2)}) copy-start(bf16[64,64]{1,0:T(8,128)(2,1)} %copy-done.15) | copy-start | bytes 24580 | tf_op jit(solution)/shard_map/while
  573.9 25.3 %copy-start.18 = (bf16[64,64]{1,0:T(8,128)(2,1)S(1)}, bf16[64,64]{1,0:T(8,128)(2,1)}, u32[]{:S(2)}) copy-start(bf16[64,64]{1,0:T(8,128)(2,1)} %copy-done.17) | copy-start | bytes 24580 | tf_op jit(solution)/shard_map/while
  605.8 15.5 %copy-start.2 = (bf16[1,1920,64]{2,1,0:T(8,128)(2,1)}, bf16[1,1920,64]{2,1,0:T(8,128)(2,1)S(1)}, u32[]{:S(2)}) copy-start(bf16[1,1920,64]{2,1,0:T(8,128)(2,1)S(1)} %get-tuple-element.530) | copy-start | bytes 737284 | tf_op jit(solution)/shard_map/while
  638.6 25.2 %copy-start.20 = (bf16[64,64]{1,0:T(8,128)(2,1)S(1)}, bf16[64,64]{1,0:T(8,128)(2,1)}, u32[]{:S(2)}) copy-start(bf16[64,64]{1,0:T(8,128)(2,1)} %copy-done.19) | copy-start | bytes 24580 | tf_op jit(solution)/shard_map/while
  638.6 25.2 %copy-start.22 = (bf16[64,64]{1,0:T(8,128)(2,1)S(1)}, bf16[64,64]{1,0:T(8,128)(2,1)}, u32[]{:S(2)}) copy-start(bf16[64,64]{1,0:T(8,128)(2,1)} %copy-done.21) | copy-start | bytes 24580 | tf_op jit(solution)/shard_map/while
  671.6 25.2 %copy-start.16 = (bf16[64,64]{1,0:T(8,128)(2,1)S(1)}, bf16[64,64]{1,0:T(8,128)(2,1)}, u32[]{:S(2)}) copy-start(bf16[64,64]{1,0:T(8,128)(2,1)} %copy-done.15) | copy-start | bytes 24580 | tf_op jit(solution)/shard_map/while
  671.6 25.2 %copy-start.18 = (bf16[64,64]{1,0:T(8,128)(2,1)S(1)}, bf16[64,64]{1,0:T(8,128)(2,1)}, u32[]{:S(2)}) copy-start(bf16[64,64]{1,0:T(8,128)(2,1)} %copy-done.17) | copy-start | bytes 24580 | tf_op jit(solution)/shard_map/while
  703.5 15.5 %copy-start.2 = (bf16[1,1920,64]{2,1,0:T(8,128)(2,1)}, bf16[1,1920,64]{2,1,0:T(8,128)(2,1)S(1)}, u32[]{:S(2)}) copy-start(bf16[1,1920,64]{2,1,0:T(8,128)(2,1)S(1)} %get-tuple-element.530) | copy-start | bytes 737284 | tf_op jit(solution)/shard_map/while
  736.3 25.2 %copy-start.20 = (bf16[64,64]{1,0:T(8,128)(2,1)S(1)}, bf16[64,64]{1,0:T(8,128)(2,1)}, u32[]{:S(2)}) copy-start(bf16[64,64]{1,0:T(8,128)(2,1)} %copy-done.19) | copy-start | bytes 24580 | tf_op jit(solution)/shard_map/while
  736.3 25.2 %copy-start.22 = (bf16[64,64]{1,0:T(8,128)(2,1)S(1)}, bf16[64,64]{1,0:T(8,128)(2,1)}, u32[]{:S(2)}) copy-start(bf16[64,64]{1,0:T(8,128)(2,1)} %copy-done.21) | copy-start | bytes 24580 | tf_op jit(solution)/shard_map/while
  769.2 25.2 %copy-start.16 = (bf16[64,64]{1,0:T(8,128)(2,1)S(1)}, bf16[64,64]{1,0:T(8,128)(2,1)}, u32[]{:S(2)}) copy-start(bf16[64,64]{1,0:T(8,128)(2,1)} %copy-done.15) | copy-start | bytes 24580 | tf_op jit(solution)/shard_map/while
  769.3 25.2 %copy-start.18 = (bf16[64,64]{1,0:T(8,128)(2,1)S(1)}, bf16[64,64]{1,0:T(8,128)(2,1)}, u32[]{:S(2)}) copy-start(bf16[64,64]{1,0:T(8,128)(2,1)} %copy-done.17) | copy-start | bytes 24580 | tf_op jit(solution)/shard_map/while
  801.1 15.5 %copy-start.2 = (bf16[1,1920,64]{2,1,0:T(8,128)(2,1)}, bf16[1,1920,64]{2,1,0:T(8,128)(2,1)S(1)}, u32[]{:S(2)}) copy-start(bf16[1,1920,64]{2,1,0:T(8,128)(2,1)S(1)} %get-tuple-element.530) | copy-start | bytes 737284 | tf_op jit(solution)/shard_map/while
  833.9 25.2 %copy-start.20 = (bf16[64,64]{1,0:T(8,128)(2,1)S(1)}, bf16[64,64]{1,0:T(8,128)(2,1)}, u32[]{:S(2)}) copy-start(bf16[64,64]{1,0:T(8,128)(2,1)} %copy-done.19) | copy-start | bytes 24580 | tf_op jit(solution)/shard_map/while
  833.9 25.2 %copy-start.22 = (bf16[64,64]{1,0:T(8,128)(2,1)S(1)}, bf16[64,64]{1,0:T(8,128)(2,1)}, u32[]{:S(2)}) copy-start(bf16[64,64]{1,0:T(8,128)(2,1)} %copy-done.21) | copy-start | bytes 24580 | tf_op jit(solution)/shard_map/while
  866.9 25.2 %copy-start.16 = (bf16[64,64]{1,0:T(8,128)(2,1)S(1)}, bf16[64,64]{1,0:T(8,128)(2,1)}, u32[]{:S(2)}) copy-start(bf16[64,64]{1,0:T(8,128)(2,1)} %copy-done.15) | copy-start | bytes 24580 | tf_op jit(solution)/shard_map/while
  866.9 25.2 %copy-start.18 = (bf16[64,64]{1,0:T(8,128)(2,1)S(1)}, bf16[64,64]{1,0:T(8,128)(2,1)}, u32[]{:S(2)}) copy-start(bf16[64,64]{1,0:T(8,128)(2,1)} %copy-done.17) | copy-start | bytes 24580 | tf_op jit(solution)/shard_map/while
  900.1 130.2 %reduce-scatter.25.cloned.1.call-start = ((), (), s32[]{:S(2)}) async-start(), calls=%async_computation.19 | async-start | bytes 1769472
  912.4 166.6 %reduce-scatter.21.cloned.1.call-start = ((), (), s32[]{:S(2)}) async-start(), calls=%async_computation.16 | async-start | bytes 5242880 | tf_op jit(solution)/shard_map/reduce_scatter | solution.py:73
  920.3 228.2 %reduce-scatter.17.cloned.1.call-start = ((), (), s32[]{:S(2)}) async-start(), calls=%async_computation.13 | async-start | bytes 5242880 | tf_op jit(solution)/shard_map/reduce_scatter | solution.py:67
  933.0 146.0 %copy-start.6 = (bf16[1,512,1024]{2,1,0:T(8,128)(2,1)S(1)}, bf16[1,512,1024]{2,1,0:T(8,128)(2,1)}, u32[]{:S(2)}) copy-start(bf16[1,512,1024]{2,1,0:T(8,128)(2,1)} %param.19) | copy-start | bytes 3145732
  933.0 146.0 %copy-start.43 = (f32[512]{0:T(512)S(1)}, f32[512]{0:T(512)}, u32[]{:S(2)}) copy-start(f32[512]{0:T(512)} %copy-done.42) | copy-start | bytes 6148
  933.0 200.4 %copy-start.24 = (f32[3,128,256]{1,2,0:T(8,128)S(1)}, f32[3,128,256]{1,2,0:T(8,128)}, u32[]{:S(2)}) copy-start(f32[3,128,256]{1,2,0:T(8,128)} %copy-done.23) | copy-start | bytes 1179652
  936.1 94.1 %copy-start.26 = (bf16[1024,128]{1,0:T(8,128)(2,1)}, bf16[1024,128]{1,0:T(8,128)(2,1)S(1)}, u32[]{:S(2)}) copy-start(bf16[1024,128]{1,0:T(8,128)(2,1)S(1)} %copy.129) | copy-start | bytes 786436
  963.0 67.2 %copy-start.33 = (bf16[256,128]{1,0:T(8,128)(2,1)}, bf16[256,128]{1,0:T(8,128)(2,1)S(1)}, u32[]{:S(2)}) copy-start(bf16[256,128]{1,0:T(8,128)(2,1)S(1)} %copy.127) | copy-start | bytes 196612
  1031.9 116.5 %copy-start.8 = (bf16[512,1024]{1,0:T(8,128)(2,1)S(1)}, bf16[512,1024]{1,0:T(8,128)(2,1)}, u32[]{:S(2)}) copy-start(bf16[512,1024]{1,0:T(8,128)(2,1)} %reduce-scatter.15.cloned.1.call-done) | copy-start | bytes 3145732
  1031.9 116.5 %copy-start.37 = (f32[512]{0:T(512)S(1)}, f32[512]{0:T(512)}, u32[]{:S(2)}) copy-start(f32[512]{0:T(512)} %copy-done.36) | copy-start | bytes 6148
  1031.9 116.5 %copy-start.39 = (f32[1024]{0:T(1024)S(1)}, f32[1024]{0:T(1024)}, u32[]{:S(2)}) copy-start(f32[1024]{0:T(1024)} %param.27) | copy-start | bytes 12292
  1032.0 116.5 %copy-start.41 = (f32[512]{0:T(512)S(1)}, f32[512]{0:T(512)}, u32[]{:S(2)}) copy-start(f32[512]{0:T(512)} %copy-done.40) | copy-start | bytes 6148
  1137.8 15.3 %copy-start.54 = (f32[128]{0:T(128)}, f32[128]{0:T(128)S(1)}, u32[]{:S(2)}) copy-start(f32[128]{0:T(128)S(1)} %add_divide_fusion.7) | copy-start | bytes 1540
  1138.4 14.7 %copy-start.55 = (f32[128]{0:T(128)}, f32[128]{0:T(128)S(1)}, u32[]{:S(2)}) copy-start(f32[128]{0:T(128)S(1)} %add_divide_fusion.6) | copy-start | bytes 1540
  (67 other events, 295.8 us)
Sparse Core Ops, SparseCore 0:
  10.7 51.6 all-gather.9
  64.5 33.2 all-gather.7
  208.6 44.5 reduce-scatter.14
  258.4 34.4 all-gather.11
  295.5 53.7 all-gather.13
  350.8 32.6 all-gather.17
  407.7 44.5 reduce-scatter.18
  458.6 34.4 all-gather.15
  496.7 67.9 reduce-scatter.28
  568.1 66.8 reduce-scatter.22
  900.2 61.8 reduce-scatter.26
  966.3 63.8 reduce-scatter.24
  1032.8 44.0 reduce-scatter.20
  1079.4 44.5 reduce-scatter.16
